TPU v7x, 32 devices: a whole 2x2x4 slice. The times are simulated.
32 devices in a mesh: tiles: 8 (over z, x), cams: 4 (over y, core).
Axes of the slice: x: 2, y: 2, z: 4, core: 2. Of those that a mesh axis runs over, the one named last changes fastest.
Arguments:
- offsets: float32 [2, 8192], P(None, ('tiles', 'cams')), may hold values from -6 to 6
- factor_diag: float32 [2, 8192], P(None, ('tiles', 'cams')), may hold values from 0.8 to 4
- factor_off: float32 [8192], P(('tiles', 'cams')), may hold values from -4 to 4
- logit: float32 [8192], P(('tiles', 'cams')), may hold values from -6 to 6
- appearance: float32 [19, 8192], P(None, ('tiles', 'cams')), may hold values from -6 to 6
- cam_linear: float32 [4, 4], P('cams'), may hold values from -0.3 to 0.3
- cam_shift: float32 [4, 2], P('cams'), may hold values from -2 to 2
- block_lists: int32 [4, 128, 2, 3], P('cams', 'tiles'), may hold values from 0 to 1023, as said below
- pix_grad: bfloat16 [19, 4, 32768], P(None, 'cams', 'tiles'), may hold values from -6 to 6
Outputs:
- rendered: float32 [19, 4, 32768], P(None, 'cams', 'tiles')
- grad_geometry: float32 [6, 8192], P(None, ('tiles', 'cams'))
- grad_appearance: float32 [19, 8192], P(None, ('tiles', 'cams'))
Inputs may be any that keep to these rules, and one draw needn't show every extreme that they name: `block_lists`: call blocks k * 128 to (k+1) * 128 - 1 column k. For each camera and each aligned run of 16 tiles (the tiles of one device), at most 24 list entries of both slabs together name blocks of one column, and exactly 24 name blocks of some column.
All inputs are finite; a program needn't handle non-finite values.
Results may differ from a plain program's by a relative error of at most 0.012.
The roundings to bfloat16 on the way count: a program that leaves them out, or rounds other values in their place, can miss the bound.
Values may be sent and summed in bfloat16 or wider, within the bound.
A program may use at most 64 MiB of HBM per device.

v0:
```python
import jax
import jax.numpy as jnp
from jax import lax
from jax.sharding import PartitionSpec as P

SIDE = 16
TPD = 16
LIST = 3
BLK = 8


def project(geometry, linear, camera_shift):
    lin_xx = 1.0 + linear[0]
    lin_xy = linear[1]
    lin_yx = linear[2]
    lin_yy = 1.0 + linear[3]
    diag_x = geometry[2]
    diag_y = geometry[3]
    lower = geometry[4]
    cov_xx = diag_x * diag_x
    cov_xy = diag_x * lower
    cov_yy = lower * lower + diag_y * diag_y
    half_xx = lin_xx * cov_xx + lin_xy * cov_xy
    half_xy = lin_xx * cov_xy + lin_xy * cov_yy
    half_yx = lin_yx * cov_xx + lin_yy * cov_xy
    half_yy = lin_yx * cov_xy + lin_yy * cov_yy
    img_xx = half_xx * lin_xx + half_xy * lin_xy + 0.3
    img_xy = half_xx * lin_yx + half_xy * lin_yy
    img_yy = half_yx * lin_yx + half_yy * lin_yy + 0.3
    determ = img_xx * img_yy - img_xy * img_xy
    centre_x = lin_xx * geometry[0] + lin_xy * geometry[1] + camera_shift[0]
    centre_y = lin_yx * geometry[0] + lin_yy * geometry[1] + camera_shift[1]
    opacity = 0.95 * jax.nn.sigmoid(geometry[5])
    return jnp.stack(
        [centre_x, centre_y, img_yy / determ, -img_xy / determ, img_xx / determ, opacity]
    )


def render_tile(projected, colours):
    pixels = jnp.arange(SIDE * SIDE)
    across = (pixels % SIDE).astype(jnp.float32) + 0.5 - SIDE / 2
    downward = (pixels // SIDE).astype(jnp.float32) + 0.5 - SIDE / 2
    delta_x = across[None, :] - projected[0][:, None]
    delta_y = downward[None, :] - projected[1][:, None]
    quadric = (
        projected[2][:, None] * delta_x * delta_x
        + 2.0 * projected[3][:, None] * delta_x * delta_y
        + projected[4][:, None] * delta_y * delta_y
    )
    coverage = projected[5][:, None] * jnp.exp(-0.5 * quadric)
    log_keep = jnp.log1p(-coverage)
    weight = jnp.exp(jnp.cumsum(log_keep, axis=0) - log_keep) * coverage
    return jnp.dot(
        colours, weight, precision=lax.Precision.HIGHEST, preferred_element_type=jnp.float32
    )


def tile_grads(projected, colours, cotangent):
    per_tile = projected.shape[1] // TPD
    channels = colours.shape[0]
    proj_tiles = projected.reshape(6, TPD, per_tile)
    colour_tiles = colours.reshape(channels, TPD, per_tile)

    def forward(proj_arg, colour_arg):
        return jax.vmap(render_tile, in_axes=(1, 1), out_axes=1)(proj_arg, colour_arg)

    picture, pullback = jax.vjp(forward, proj_tiles, colour_tiles)
    grad_proj, grad_colour = pullback(cotangent)
    return (picture, grad_proj.reshape(6, -1), grad_colour.reshape(channels, -1))


def slot_ranks(entries, blocks_per_column, columns):
    column = entries // blocks_per_column
    in_column = entries % blocks_per_column
    matches = (column[..., None] == jnp.arange(columns, dtype=jnp.int32)).astype(jnp.int32)
    before = jnp.cumsum(matches, axis=-2) - matches
    ranking = jnp.sum(before * matches, axis=-1)
    return (column, ranking, in_column)


def local(
    offsets,
    factor_diag,
    factor_off,
    logit,
    appearance,
    cam_linear,
    cam_shift,
    block_lists,
    pix_grad,
):
    columns = lax.axis_size("tiles")
    capacity = 4 * TPD * LIST // columns
    slot_count = columns * capacity
    channels = appearance.shape[0]
    geometry = jnp.concatenate([offsets, factor_diag, factor_off[None, :], logit[None, :]], axis=0)
    geometry_col, appearance_col = (
        lax.all_gather(geometry, "cams", axis=1, tiled=True),
        lax.all_gather(appearance, "cams", axis=1, tiled=True),
    )
    per_column = geometry_col.shape[1] // BLK
    linear = cam_linear[0]
    camera_shift = cam_shift[0]
    entries = block_lists.reshape(-1)
    entry_count = entries.shape[0]
    column, ranking, in_column = slot_ranks(entries, per_column, columns)
    entry_slot = column * capacity + ranking
    request = jnp.zeros((slot_count,), jnp.int32).at[entry_slot].set(in_column)
    wanted = lax.all_to_all(request, "tiles", split_axis=0, concat_axis=0, tiled=True)
    raw_params = geometry_col.reshape(6, per_column, BLK)[:, wanted].reshape(6, slot_count * BLK)
    raw_colours = appearance_col.reshape(channels, per_column, BLK)[:, wanted].reshape(
        channels, slot_count * BLK
    )
    send_proj = project(raw_params, linear, camera_shift).astype(jnp.bfloat16)
    got_proj, got_colour = (
        lax.all_to_all(send_proj, "tiles", split_axis=1, concat_axis=1, tiled=True),
        lax.all_to_all(
            raw_colours.astype(jnp.bfloat16), "tiles", split_axis=1, concat_axis=1, tiled=True
        ),
    )
    projected = (
        got_proj.reshape(6, slot_count, BLK)[:, entry_slot]
        .reshape(6, entry_count * BLK)
        .astype(jnp.float32)
    )
    colours = (
        got_colour.reshape(channels, slot_count, BLK)[:, entry_slot]
        .reshape(channels, entry_count * BLK)
        .astype(jnp.float32)
    )
    cotangent = pix_grad.reshape(channels, TPD, -1).astype(jnp.float32)
    picture, grad_proj, grad_colour = tile_grads(projected, colours, cotangent)
    back_proj = (
        jnp.zeros((6, slot_count, BLK), jnp.bfloat16)
        .at[:, entry_slot]
        .set(grad_proj.reshape(6, entry_count, BLK).astype(jnp.bfloat16))
    )
    back_colour = (
        jnp.zeros((channels, slot_count, BLK), jnp.bfloat16)
        .at[:, entry_slot]
        .set(grad_colour.reshape(channels, entry_count, BLK).astype(jnp.bfloat16))
    )
    ret_proj, ret_colour = (
        lax.all_to_all(back_proj.reshape(6, -1), "tiles", split_axis=1, concat_axis=1, tiled=True),
        lax.all_to_all(
            back_colour.reshape(channels, -1), "tiles", split_axis=1, concat_axis=1, tiled=True
        ),
    )
    unused, pull_params = jax.vjp(lambda params: project(params, linear, camera_shift), raw_params)
    grad_raw = pull_params(ret_proj.astype(jnp.float32))[0]
    owner_hot = (wanted[:, None] == jnp.arange(per_column, dtype=jnp.int32)[None, :]).astype(
        jnp.float32
    )

    def collect(values, row_count):
        summed = jnp.einsum(
            "rsb,sk->rkb",
            values.reshape(row_count, slot_count, BLK),
            owner_hot,
            precision=lax.Precision.HIGHEST,
        )
        return summed.reshape(row_count, per_column * BLK)

    column_geometry = collect(grad_raw, 6)
    column_colour = collect(ret_colour.astype(jnp.float32), channels)
    grad_geometry, grad_appearance = (
        lax.psum_scatter(column_geometry, "cams", scatter_dimension=1, tiled=True),
        lax.psum_scatter(column_colour, "cams", scatter_dimension=1, tiled=True),
    )
    return (picture.reshape(channels, 1, -1), grad_geometry, grad_appearance)


def solution(mesh):
    return jax.shard_map(
        local,
        mesh=mesh,
        in_specs=(
            P(None, ("tiles", "cams")),
            P(None, ("tiles", "cams")),
            P(("tiles", "cams")),
            P(("tiles", "cams")),
            P(None, ("tiles", "cams")),
            P("cams", None),
            P("cams", None),
            P("cams", "tiles", None, None),
            P(None, "cams", "tiles"),
        ),
        out_specs=(
            P(None, "cams", "tiles"),
            P(None, ("tiles", "cams")),
            P(None, ("tiles", "cams")),
        ),
        check_vma=False,
    )
```

profile of v0, /device:TPU:0, one launch (start us, length us, event | category | flops | bytes accessed | tf_op | source)
XLA Modules:
  0.0 147.2 jit_solution(7132436189232123413)
XLA Ops:
  10.2 7.3 %all-to-all-start = ((s32[8,24,1]{1,2,0:T(1,128)}), s32[8,24,1]{1,2,0:T(1,128)S(1)}, u32[]{:S(2)}, u32[]{:S(2)}) async-start(s32[8,24,1]{1,2,0:T(1,128)} %bitcast.3), calls=%async_computation | async-start | bytes 8192 | tf_op jit(solution)/shard_map/all_to_all | solution.py:109
  17.4 1.5 %fusion.57 = (f32[1,1]{1,0:T(1,128)}, f32[1,1]{1,0:T(1,128)}, f32[1,1]{1,0:T(1,128)}, f32[1,1]{1,0:T(1,128)}) fusion(f32[1,4]{1,0:T(1,128)} %param.14), kind=kLoop, calls=%fused_computation.165 | loop fusion | bytes 32 | tf_op jit(solution)/shard_map/slice | solution.py:15
  18.9 1.3 fusion.58
  21.0 5.2 %all_gather.6 = bf16[19,1024]{1,0:T(8,128)(2,1)S(1)} all-gather(bf16[19,256]{1,0:T(8,128)(2,1)S(1)} %convert.43), channel_id=1, replica_groups=mesh['tiles'=8,'cams'=4] {'cams'}, dimensions={1}, use_global_device_ids=true | all-gather | bytes 48640 | tf_op jit(solution)/shard_map/all_gather | solution.py:99
  26.9 5.2 %all_gather.7 = f32[6,1024]{1,0:T(8,128)S(1)} all-gather(f32[6,256]{1,0:T(8,128)S(1)} %pad_maximum_fusion), channel_id=1, replica_groups=mesh['tiles'=8,'cams'=4] {'cams'}, dimensions={1}, use_global_device_ids=true | all-gather | bytes 30720 | tf_op jit(solution)/shard_map/all_gather | solution.py:98
  36.6 1.3 slice_add_fusion
  37.9 2.6 %add_convert_fusion.1 = (bf16[1,192,8]{1,2,0:T(8,128)(2,1)S(1)}, bf16[1,192,8]{1,2,0:T(8,128)(2,1)S(1)}) fusion(f32[6,192,8]{1,2,0:T(8,128)S(1)} %bitcast.89, f32[]{:T(128)} %bitcast.18, f32[]{:T(128)} %bitcast.17, f32[]{:T(128)} %bitcast.16, f32[]{:T(128)} %bitcast.15, f32[]{:T(128)} %bitcast.14, f32[]{:T(128)} %bitcast.10), kind=kLoop, calls=%fused_computation.115 | loop fusion | flops 15360 | bytes 18456 | tf_op jit(solution)/shard_map/convert.6
  42.7 6.0 %all-to-all-start.2 = ((bf16[6,8,192]{2,0,1:T(8,128)(2,1)}), bf16[6,8,192]{2,0,1:T(8,128)(2,1)S(1)}, u32[]{:S(2)}, u32[]{:S(2)}) async-start(bf16[6,8,192]{2,0,1:T(8,128)(2,1)} %copy.86), calls=%async_computation.2 | async-start | bytes 65536 | tf_op jit(solution)/shard_map/all_to_all | solution.py:116
  52.2 3.2 %all-to-all-done.2 = bf16[6,8,192]{2,0,1:T(8,128)(2,1)S(1)} async-done(((bf16[6,8,192]{2,0,1:T(8,128)(2,1)}), bf16[6,8,192]{2,0,1:T(8,128)(2,1)S(1)}, u32[]{:S(2)}, u32[]{:S(2)}) %all-to-all-start.2) | async-done | bytes 18464 | tf_op jit(solution)/shard_map/all_to_all | solution.py:116
  55.4 3.4 %all-to-all-start.1 = ((bf16[19,8,192]{2,0,1:T(8,128)(2,1)}), bf16[19,8,192]{2,0,1:T(8,128)(2,1)S(1)}, u32[]{:S(2)}, u32[]{:S(2)}) async-start(bf16[19,8,192]{2,0,1:T(8,128)(2,1)} %copy.75), calls=%async_computation.1 | async-start | bytes 196608 | tf_op jit(solution)/shard_map/all_to_all | solution.py:117
  62.6 1.8 %fusion = bf16[19,16,48]{2,0,1:T(8,128)(2,1)S(1)} fusion(f32[16,48]{1,0:T(8,128)S(1)} %mul.1397, f32[16,48]{1,0:T(8,128)S(1)} %sub.116, f32[256]{0:T(256)S(1)} %get-tuple-element.70, f32[16,48]{1,0:T(8,128)S(1)} %mul.1393, f32[16,48]{1,0:T(8,128)S(1)} %sub.110, f32[256]{0:T(256)S(1)} %get-tuple-element.71, f32[16,48]{1,0:T(8,128)S(1)} %mul.1388, ...), kind=kOutput, calls=%fused_computation.20 | convolution fusion | flops 47790336 | bytes 991744 | tf_op jit(solution)/shard_map/transpose(jvp(vmap()))/dot_general | solution.py:53
  64.7 3.4 %scatter_fusion.1 = bf16[19,192,8]{0,2,1:T(8,128)(2,1)S(1)} fusion(bf16[19,192,8]{0,2,1:T(8,128)(2,1)S(1)} %broadcast_in_dim.20, s32[96]{0:T(128)S(1)} %fusion.48, bf16[96,19,8]{1,2,0:T(8,128)(2,1)S(1)} %bitcast.80), kind=kCustom, calls=%fused_computation.6 | custom fusion | bytes 87936 | tf_op jit(solution)/shard_map/scatter | solution.py:141
  68.9 5.9 %all-to-all-start.4 = ((bf16[19,8,192]{2,0,1:T(8,128)(2,1)}), bf16[19,8,192]{2,0,1:T(8,128)(2,1)S(1)}, u32[]{:S(2)}, u32[]{:S(2)}) async-start(bf16[19,8,192]{2,0,1:T(8,128)(2,1)} %copy.108), calls=%async_computation.5 | async-start | bytes 196608 | tf_op jit(solution)/shard_map/all_to_all | solution.py:145
  77.8 2.9 %fusion.14 = (f32[16,48]{1,0:T(8,128)S(1)}, f32[16,48]{1,0:T(8,128)S(1)}, f32[16,48]{1,0:T(8,128)S(1)}, f32[16,48]{1,0:T(8,128)S(1)}, f32[16,48]{1,0:T(8,128)S(1)}, /*index=5*/f32[16,48]{1,0:T(8,128)S(1)}) fusion(f32[16,48]{1,0:T(8,128)S(1)} %sub.116, f32[256]{0:T(256)S(1)} %get-tuple-element.70, f32[16,48]{1,0:T(8,128)S(1)} %mul.1397, ...), kind=kLoop, calls=%fused_computation.36 | loop fusion | flops 9432576 | bytes 2398208 | tf_op jit(solution)/shard_map/transpose(jvp(vmap()))/reduce_sum | solution.py:48
  81.1 3.4 %scatter_fusion = bf16[6,192,8]{2,0,1:T(8,128)(2,1)S(1)} fusion(bf16[6,192,8]{2,0,1:T(8,128)(2,1)S(1)} %broadcast_in_dim.16, s32[96]{0:T(128)S(1)} %fusion.48, bf16[96,6,8]{2,1,0:T(8,128)(2,1)S(1)} %copy.97), kind=kCustom, calls=%fused_computation.5 | custom fusion | bytes 28032 | tf_op jit(solution)/shard_map/scatter | solution.py:136
  85.4 6.0 %all-to-all-start.3 = ((bf16[6,8,192]{2,0,1:T(8,128)(2,1)}), bf16[6,8,192]{2,0,1:T(8,128)(2,1)S(1)}, u32[]{:S(2)}, u32[]{:S(2)}) async-start(bf16[6,8,192]{2,0,1:T(8,128)(2,1)} %copy.99), calls=%async_computation.3 | async-start | bytes 65536 | tf_op jit(solution)/shard_map/all_to_all | solution.py:144
  93.1 5.0 %all-to-all-done.3 = bf16[6,8,192]{2,0,1:T(8,128)(2,1)S(1)} async-done(((bf16[6,8,192]{2,0,1:T(8,128)(2,1)}), bf16[6,8,192]{2,0,1:T(8,128)(2,1)S(1)}, u32[]{:S(2)}, u32[]{:S(2)}) %all-to-all-start.3) | async-done | bytes 18464 | tf_op jit(solution)/shard_map/all_to_all | solution.py:144
  98.1 1.4 fusion.38
  100.2 1.3 negate_add_fusion
  101.5 1.3 multiply_add_fusion.4
  105.4 1.5 %convolution_bitcast_fusion = f32[19,16,256]{2,0,1:T(8,128)S(1)} fusion(bf16[19,16,48]{0,2,1:T(8,128)(2,1)S(1)} %bitcast.85, f32[16,48]{1,0:T(8,128)S(1)} %mul.1397, f32[16,48]{1,0:T(8,128)S(1)} %sub.116, f32[256]{0:T(256)S(1)} %get-tuple-element.70, f32[16,48]{1,0:T(8,128)S(1)} %mul.1393, f32[16,48]{1,0:T(8,128)S(1)} %sub.110, ...), kind=kOutput, calls=%fused_computation.18 | convolution fusion | flops 47775744 | bytes 1147392 | tf_op jit(solution)/shard_map/jvp(vmap())/dot_general | solution.py:53
  108.1 9.7 %reduce-scatter.5.cloned.1.call-done = f32[19,256]{0,1:T(8,128)} async-done(((f32[19,1024]{0,1:T(8,128)}), f32[19,256]{0,1:T(8,128)}) %reduce-scatter.5.cloned.1.call-update) | async-done | bytes 19472 | tf_op jit(solution)/shard_map/reduce_scatter | solution.py:168
  117.8 1.6 %copy.113 = f32[19,256]{1,0:T(8,128)} copy(f32[19,256]{0,1:T(8,128)} %reduce-scatter.5.cloned.1.call-done) | data formatting | bytes 38912
  119.4 21.0 %reduce-scatter.3.cloned.1.call-done = f32[6,256]{1,0:T(8,128)} async-done(((f32[6,1024]{1,0:T(8,128)}), f32[6,256]{1,0:T(8,128)}) %reduce-scatter.3.cloned.1.call-update) | async-done | bytes 6160 | tf_op jit(solution)/shard_map/reduce_scatter | solution.py:167
  (125 shorter events, 28.2 us)
Async XLA Ops:
  8.4 25.4 %copy-start = (bf16[19,1,4096]{2,0,1:T(8,128)(2,1)S(1)}, bf16[19,1,4096]{2,0,1:T(8,128)(2,1)}, u32[]{:S(2)}) copy-start(bf16[19,1,4096]{2,0,1:T(8,128)(2,1)} %param.17) | copy-start | bytes 466948
  10.2 24.0 %all-to-all-start = ((s32[8,24,1]{1,2,0:T(1,128)}), s32[8,24,1]{1,2,0:T(1,128)S(1)}, u32[]{:S(2)}, u32[]{:S(2)}) async-start(s32[8,24,1]{1,2,0:T(1,128)} %bitcast.3), calls=%async_computation | async-start | bytes 8192 | tf_op jit(solution)/shard_map/all_to_all | solution.py:109
  42.7 12.7 %all-to-all-start.2 = ((bf16[6,8,192]{2,0,1:T(8,128)(2,1)}), bf16[6,8,192]{2,0,1:T(8,128)(2,1)S(1)}, u32[]{:S(2)}, u32[]{:S(2)}) async-start(bf16[6,8,192]{2,0,1:T(8,128)(2,1)} %copy.86), calls=%async_computation.2 | async-start | bytes 65536 | tf_op jit(solution)/shard_map/all_to_all | solution.py:116
  55.4 13.5 %all-to-all-start.1 = ((bf16[19,8,192]{2,0,1:T(8,128)(2,1)}), bf16[19,8,192]{2,0,1:T(8,128)(2,1)S(1)}, u32[]{:S(2)}, u32[]{:S(2)}) async-start(bf16[19,8,192]{2,0,1:T(8,128)(2,1)} %copy.75), calls=%async_computation.1 | async-start | bytes 196608 | tf_op jit(solution)/shard_map/all_to_all | solution.py:117
  68.9 16.5 %all-to-all-start.4 = ((bf16[19,8,192]{2,0,1:T(8,128)(2,1)}), bf16[19,8,192]{2,0,1:T(8,128)(2,1)S(1)}, u32[]{:S(2)}, u32[]{:S(2)}) async-start(bf16[19,8,192]{2,0,1:T(8,128)(2,1)} %copy.108), calls=%async_computation.5 | async-start | bytes 196608 | tf_op jit(solution)/shard_map/all_to_all | solution.py:145
  85.4 12.7 %all-to-all-start.3 = ((bf16[6,8,192]{2,0,1:T(8,128)(2,1)}), bf16[6,8,192]{2,0,1:T(8,128)(2,1)S(1)}, u32[]{:S(2)}, u32[]{:S(2)}) async-start(bf16[6,8,192]{2,0,1:T(8,128)(2,1)} %copy.99), calls=%async_computation.3 | async-start | bytes 65536 | tf_op jit(solution)/shard_map/all_to_all | solution.py:144
  91.4 26.4 %reduce-scatter.5.cloned.1.call-start = ((), (), s32[]{:S(2)}) async-start(), calls=%async_computation.8 | async-start | bytes 655360 | tf_op jit(solution)/shard_map/reduce_scatter | solution.py:168
  93.0 47.3 %reduce-scatter.3.cloned.1.call-start = ((), (), s32[]{:S(2)}) async-start(), calls=%async_computation.7 | async-start | bytes 40960 | tf_op jit(solution)/shard_map/reduce_scatter | solution.py:167
Sparse Core Ops, SparseCore 0:
  94.7 23.0 reduce-scatter.4
  120.9 19.3 reduce-scatter.2
where the time goes:
time: 148 us; the launch traced here: 147 us
  waiting for transfers between devices  38.9 us (26%)
  local copies, waits for them, and re-layouts  30.4 us (21%)
  starting transfers between devices  28.6 us (19%)
  other arithmetic  18 us (12%)
  between operations  15.9 us (11%)
  blocking collectives  10.4 us (7%)
  matrix products  4.99 us (3%)
    reduce_scatter x1, waiting for transfers between devices, local(): lax.psum_scatter(column_geometry, 'cams', scatter_dimension=1, tiled=True)  21 us
    reduce_scatter x1, waiting for transfers between devices, local(): lax.psum_scatter(column_colour, 'cams', scatter_dimension=1, tiled=True)  9.74 us
    all_to_all x1, starting transfers between devices, local(): lax.all_to_all(request, 'tiles', split_axis=0, concat_axis=0, tiled=True)  7.25 us
    all_to_all x1, starting transfers between devices, local(): lax.all_to_all(back_proj.reshape(6, -1), 'tiles', split_axis=1, concat_ax...  6 us
    all_to_all x1, starting transfers between devices, local(): lax.all_to_all(send_proj, 'tiles', split_axis=1, concat_axis=1, tiled=True)  6 us
    all_to_all x1, starting transfers between devices, local(): lax.all_to_all(back_colour.reshape(channels, -1), 'tiles', split_axis=1,...  5.93 us
    all_gather x1, blocking collectives, local(): lax.all_gather(appearance, 'cams', axis=1, tiled=True)  5.21 us
    all_gather x1, blocking collectives, local(): lax.all_gather(geometry, 'cams', axis=1, tiled=True)  5.19 us
  transfers between devices with their start and end apart: 7, of which 4 were waited for; matrix products, arithmetic and copies ran while one was open for 28% of the time, Pallas kernels for 0%

commit v1 on v0

v1 whole, which is shorter than its diff:
```python
import functools

import jax
import jax.numpy as jnp
from jax import lax
from jax.experimental import pallas as pl
from jax.experimental.pallas import tpu as pltpu
from jax.sharding import PartitionSpec as P

SIDE = 16
TPD = 16
LIST = 3
BLK = 8
PIX = SIDE * SIDE
LANES = 128
PAR = 32
GEO = 24
STEPS = 2 * LIST * BLK
ROWS = BLK * LANES
MESH = pl.DeviceIdType.MESH
F32 = jnp.float32
BF16 = jnp.bfloat16

NN = (((1,), (0,)), ((), ()))
NT = (((1,), (1,)), ((), ()))
TN = (((0,), (0,)), ((), ()))


def dot(a, b, dims):
    return lax.dot_general(a, b, dims, preferred_element_type=F32)


def iota(shape, dim):
    return lax.broadcasted_iota(jnp.int32, shape, dim)


def rounded(values):
    return values.astype(BF16).astype(F32)


def split(values):
    high = rounded(values)
    rest = values - high
    middle = rounded(rest)
    return high, middle, rest - middle


def project(offset_x, offset_y, diag_x, diag_y, lower, logit, linear, camera_shift):
    lin_xx = 1.0 + linear[0]
    lin_xy = linear[1]
    lin_yx = linear[2]
    lin_yy = 1.0 + linear[3]
    cov_xx = diag_x * diag_x
    cov_xy = diag_x * lower
    cov_yy = lower * lower + diag_y * diag_y
    half_xx = lin_xx * cov_xx + lin_xy * cov_xy
    half_xy = lin_xx * cov_xy + lin_xy * cov_yy
    half_yx = lin_yx * cov_xx + lin_yy * cov_xy
    half_yy = lin_yx * cov_xy + lin_yy * cov_yy
    img_xx = half_xx * lin_xx + half_xy * lin_xy + 0.3
    img_xy = half_xx * lin_yx + half_xy * lin_yy
    img_yy = half_yx * lin_yx + half_yy * lin_yy + 0.3
    determ = img_xx * img_yy - img_xy * img_xy
    centre_x = lin_xx * offset_x + lin_xy * offset_y + camera_shift[0]
    centre_y = lin_yx * offset_x + lin_yy * offset_y + camera_shift[1]
    opacity = 0.95 * jax.nn.sigmoid(logit)
    return (centre_x, centre_y, img_yy / determ, -img_xy / determ, img_xx / determ, opacity)


def kernel(
    tiles,
    cams,
    cap,
    feat,
    params_ref,
    ids_ref,
    linear_ref,
    shift_ref,
    cot_ref,
    picture_ref,
    grads_ref,
    column,
    request_out,
    request_in,
    table_out,
    table_in,
    back_out,
    back_in,
    sums_out,
    sums_in,
    cot,
    lane_sum,
    alpha,
    weight,
    dweight,
    send_cam,
    recv_cam,
    send_req,
    recv_req,
    send_tab,
    recv_tab,
    send_back,
    recv_back,
    send_sum,
    recv_sum,
):
    tile = lax.axis_index("tiles")
    cam = lax.axis_index("cams")
    own = params_ref.shape[1] // BLK
    lanes = own * BLK
    blocks = cams * own
    slots = tiles * cap

    def turn(base, k, size):
        return lax.rem(base + k + size, size)

    barrier = pltpu.get_barrier_semaphore()

    def greet_tiles(k, carry):
        pl.semaphore_signal(
            barrier, inc=1, device_id=(turn(tile, k, tiles), cam), device_id_type=MESH
        )
        return carry

    def greet_cams(k, carry):
        pl.semaphore_signal(
            barrier, inc=1, device_id=(tile, turn(cam, k, cams)), device_id_type=MESH
        )
        return carry

    lax.fori_loop(1, tiles, greet_tiles, 0)
    lax.fori_loop(1, cams, greet_cams, 0)

    ids = ids_ref[...]
    entry_column = lax.div(ids, jnp.int32(blocks))
    in_column = ids - entry_column * blocks
    entry_column = jnp.where(ids < 0, -1, entry_column)
    matches = jnp.where(entry_column == iota((tiles, LANES), 0), 1.0, 0.0)
    earlier = jnp.where(iota((LANES, LANES), 0) < iota((LANES, LANES), 1), 1.0, 0.0)
    before = dot(matches.astype(BF16), earlier.astype(BF16), NN)
    rank = jnp.sum(before * matches, axis=0, keepdims=True).astype(jnp.int32)
    slot = jnp.where(ids < 0, -1, entry_column * cap + rank)
    slot_hot = jnp.where(slot == iota((slots, LANES), 0), 1.0, 0.0).astype(BF16)
    block_hot = jnp.where(in_column == iota((blocks, LANES), 0), 1.0, 0.0).astype(BF16)
    request_out[...] = dot(slot_hot, block_hot, NT).astype(BF16).reshape(tiles, cap, blocks)

    def cam_copy(source, target, k, sends, recvs):
        return pltpu.make_async_remote_copy(
            src_ref=source,
            dst_ref=target,
            send_sem=sends.at[k],
            recv_sem=recvs.at[k],
            device_id=(tile, turn(cam, k, cams)),
            device_id_type=MESH,
        )

    def tile_copy(source, target, k, sends, recvs):
        peer = turn(tile, k, tiles)
        return pltpu.make_async_remote_copy(
            src_ref=source.at[peer],
            dst_ref=target.at[tile],
            send_sem=sends.at[k],
            recv_sem=recvs.at[k],
            device_id=(peer, cam),
            device_id_type=MESH,
        )

    def over(size, make, what):
        def step(k, carry):
            getattr(make(k), what)()
            return carry

        lax.fori_loop(1, size, step, 0)

    copy_params = lambda k: cam_copy(params_ref, column.at[cam], k, send_cam, recv_cam)
    copy_request = lambda k: tile_copy(request_out, request_in, k, send_req, recv_req)
    copy_table = lambda k: tile_copy(table_out, table_in, k, send_tab, recv_tab)
    copy_back = lambda k: tile_copy(back_out, back_in, k, send_back, recv_back)
    copy_sums = lambda k: cam_copy(
        sums_out.at[turn(cam, k, cams)], sums_in.at[cam], k, send_sum, recv_sum
    )

    pl.semaphore_wait(barrier, tiles - 1 + cams - 1)
    over(cams, copy_params, "start")
    over(tiles, copy_request, "start")
    column[cam] = params_ref[...]
    request_in[tile] = request_out[tile]

    fill = jnp.zeros((PAR - feat, PIX), F32)
    for t in range(TPD):
        part = cot_ref[:, t * PIX : (t + 1) * PIX].astype(F32)
        cot[t * PAR : (t + 1) * PAR] = jnp.concatenate([part, fill], axis=0).astype(BF16)
    pixel = iota((1, PIX), 1)
    across = (pixel & (SIDE - 1)).astype(F32) + (0.5 - SIDE / 2)
    downward = lax.div(pixel, jnp.int32(SIDE)).astype(F32) + (0.5 - SIDE / 2)
    one = jnp.ones((1, PIX), F32)
    none = jnp.zeros((2, PIX), F32)
    mono = jnp.concatenate(
        [one, across, downward, across * across, across * downward, downward * downward, none],
        axis=0,
    )
    mono_three = jnp.concatenate([mono, mono, mono, jnp.zeros((8, PIX), F32)], axis=0).astype(BF16)
    mono_one = jnp.concatenate([mono, jnp.zeros((8, PIX), F32)], axis=0).astype(BF16)
    spread = jnp.where(
        (iota((PAR, TPD * PAR), 1) & (PAR - 1)) == iota((PAR, TPD * PAR), 0), 1.0, 0.0
    ).astype(BF16)

    over(cams, copy_params, "wait_recv")
    split_rows = GEO + 3 * (PAR - GEO)
    in_block = iota((split_rows, BLK, lanes), 2) & (BLK - 1)
    in_place = in_block == iota((split_rows, BLK, lanes), 1)
    table = jnp.zeros((split_rows * BLK, blocks), F32)
    for c in range(cams):
        piece = column[c]
        stacked = jnp.concatenate([piece[:GEO], *split(piece[GEO:])], axis=0)
        apart = jnp.where(in_place, jnp.broadcast_to(stacked[:, None, :], in_place.shape), 0.0)
        apart = apart.reshape(split_rows * BLK, lanes).astype(BF16)
        to_block = jnp.where(
            iota((lanes, blocks), 1) == c * own + lax.div(iota((lanes, blocks), 0), jnp.int32(BLK)),
            1.0,
            0.0,
        ).astype(BF16)
        table = table + dot(apart, to_block, NN)
    geo_rows = (PAR - GEO) * BLK
    base = GEO * BLK
    geometry = (
        table[base : base + geo_rows]
        + table[base + geo_rows : base + 2 * geo_rows]
        + table[base + 2 * geo_rows :]
    )
    geometry = [geometry[r * BLK : (r + 1) * BLK] for r in range(6)]
    linear = [linear_ref[0, i] for i in range(4)]
    camera_shift = [shift_ref[0, i] for i in range(2)]
    projected, pull_params = jax.vjp(lambda *rows: project(*rows, linear, camera_shift), *geometry)
    table = jnp.concatenate(
        [table[:base], *projected, jnp.zeros((2 * BLK, blocks), F32)], axis=0
    ).astype(BF16)

    over(tiles, copy_request, "wait_recv")
    wanted = request_in[...].reshape(slots, blocks)
    table_out[...] = dot(wanted, table, NT).astype(BF16).reshape(tiles, cap, PAR * BLK)
    over(tiles, copy_table, "start")
    table_in[tile] = table_out[tile]
    empty = jnp.zeros((2 * TPD, PIX), F32)
    for g in range(BLK):
        row = g * LANES + 2 * LIST * TPD
        weight[row : row + 2 * TPD] = empty
        dweight[row : row + 2 * TPD] = empty
    over(tiles, copy_table, "wait_recv")

    lane_sum[...] = dot(table_in[...].reshape(slots, PAR * BLK), slot_hot, TN)
    copies = jnp.concatenate([lane_sum[pl.ds(g, PAR, stride=BLK), :] for g in range(BLK)], axis=1)
    same_tile = (iota((TPD, 1, ROWS), 2) & (TPD - 1)) == iota((TPD, 1, ROWS), 0)
    u_x, u_y, con_x, con_m, con_y, opacity = [
        copies[GEO + r : GEO + r + 1] for r in range(6)
    ]
    opacity = jnp.where(opacity > 0.0, opacity, 1.0)
    slope_x = con_x * u_x + con_m * u_y
    slope_y = con_m * u_x + con_y * u_y
    poly = jnp.concatenate(
        [
            jnp.log(opacity) - 0.5 * (slope_x * u_x + slope_y * u_y),
            slope_x,
            slope_y,
            -0.5 * con_x,
            -con_m,
            -0.5 * con_y,
            jnp.zeros((2, ROWS), F32),
        ],
        axis=0,
    )
    poly = jnp.concatenate([*split(poly), jnp.zeros((8, ROWS), F32)], axis=0).astype(BF16)
    alpha[...] = dot(poly, mono_three, TN)
    keep = jnp.ones((TPD, PIX), F32)
    order = [g * LANES + j * TPD for j in range(2 * LIST) for g in range(BLK)]
    for row in order:
        cover = jnp.exp(alpha[row : row + TPD])
        share = keep * cover
        keep = keep - share
        alpha[row : row + TPD] = cover
        weight[row : row + TPD] = share

    colour_rows = dot(copies.T.astype(BF16), spread, NN)
    own_tile = lax.div(iota((ROWS, TPD * PAR), 1), jnp.int32(PAR)) == (
        iota((ROWS, TPD * PAR), 0) & (TPD - 1)
    )
    colour_rows = jnp.where(own_tile, colour_rows, 0.0).astype(BF16)
    dweight_all = dot(colour_rows, cot[...], NN)
    behind = jnp.zeros((TPD, PIX), F32)
    for row in reversed(order):
        gap = dweight_all[row : row + TPD] - behind
        dweight[row : row + TPD] = weight[row : row + TPD] * gap
        behind = behind + alpha[row : row + TPD] * gap

    shares = weight[...].astype(BF16)
    pulled = dweight[...]
    pulled_high = pulled.astype(BF16)
    pulled_low = (pulled - pulled_high.astype(F32)).astype(BF16)
    moment = dot(mono_one, pulled_high, NT) + dot(mono_one, pulled_low, NT)
    m_0, m_x, m_y, m_xx, m_xy, m_yy = [moment[r : r + 1] for r in range(6)]
    s_x = m_x - u_x * m_0
    s_y = m_y - u_y * m_0
    s_xx = m_xx - u_x * (m_x + s_x)
    s_xy = m_xy - u_x * m_y - u_y * s_x
    s_yy = m_yy - u_y * (m_y + s_y)
    by_tile = dot(cot[...], shares, NT).reshape(TPD, PAR, ROWS)
    colour_grads = jnp.sum(jnp.where(same_tile, by_tile, 0.0), axis=0)
    copy_grads = jnp.concatenate(
        [
            colour_grads[:GEO],
            con_x * s_x + con_m * s_y,
            con_m * s_x + con_y * s_y,
            -0.5 * s_xx,
            -s_xy,
            -0.5 * s_yy,
            m_0 / opacity,
            jnp.zeros((2, ROWS), F32),
        ],
        axis=0,
    )
    for g in range(BLK):
        lane_sum[pl.ds(g, PAR, stride=BLK), :] = copy_grads[:, g * LANES : (g + 1) * LANES]
    back = dot(slot_hot, lane_sum[...].astype(BF16), NT)
    back_out[...] = back.astype(BF16).reshape(tiles, cap, PAR * BLK)
    over(tiles, copy_back, "start")
    back_in[tile] = back_out[tile]

    masked = jnp.where(same_tile, jnp.broadcast_to(copies[None], (TPD, PAR, ROWS)), 0.0)
    picture = dot(masked.reshape(TPD * PAR, ROWS).astype(BF16), shares, NN)
    for t in range(TPD):
        picture_ref[:, t * PIX : (t + 1) * PIX] = picture[t * PAR : t * PAR + feat]

    over(tiles, copy_back, "wait_recv")
    summed = dot(back_in[...].reshape(slots, PAR * BLK), wanted, TN)
    pulled_geo = pull_params(
        tuple(summed[base + r * BLK : base + (r + 1) * BLK] for r in range(6))
    )
    block_grads = jnp.concatenate(
        [summed[:base], *pulled_geo, jnp.zeros((2 * BLK, blocks), F32)], axis=0
    )
    parts = jnp.concatenate(split(block_grads), axis=0).astype(BF16)
    place = iota((PAR, lanes), 1) & (BLK - 1)
    for c in range(cams):
        from_block = jnp.where(
            iota((blocks, lanes), 0) == c * own + lax.div(iota((blocks, lanes), 1), jnp.int32(BLK)),
            1.0,
            0.0,
        ).astype(BF16)
        apart = dot(parts, from_block, NN)
        rows = PAR * BLK
        apart = apart[:rows] + apart[rows : 2 * rows] + apart[2 * rows :]
        apart = apart.reshape(PAR, BLK, lanes)
        chosen = jnp.where(
            (iota((PAR, BLK, lanes), 2) & (BLK - 1)) == iota((PAR, BLK, lanes), 1), apart, 0.0
        )
        sums_out[c] = jnp.sum(chosen, axis=1)
    over(cams, copy_sums, "start")
    sums_in[cam] = sums_out[cam]
    over(cams, copy_sums, "wait_recv")
    grads_ref[...] = jnp.sum(sums_in[...], axis=0)

    over(cams, copy_params, "wait_send")
    over(tiles, copy_request, "wait_send")
    over(tiles, copy_table, "wait_send")
    over(tiles, copy_back, "wait_send")
    over(cams, copy_sums, "wait_send")


def local(
    offsets,
    factor_diag,
    factor_off,
    logit,
    appearance,
    cam_linear,
    cam_shift,
    block_lists,
    pix_grad,
):
    tiles = lax.axis_size("tiles")
    cams = lax.axis_size("cams")
    channels = appearance.shape[0]
    lanes = offsets.shape[1]
    blocks = cams * lanes // BLK
    cap = -(-(4 * TPD * LIST // tiles) // 16) * 16
    params = jnp.concatenate(
        [
            appearance,
            jnp.zeros((GEO - channels, lanes), F32),
            offsets,
            factor_diag,
            factor_off[None, :],
            logit[None, :],
            jnp.zeros((PAR - GEO - 6, lanes), F32),
        ],
        axis=0,
    )
    ids = block_lists.reshape(TPD, 2 * LIST).T.reshape(1, TPD * 2 * LIST)
    ids = jnp.pad(ids, ((0, 0), (0, LANES - ids.shape[1])), constant_values=-1)
    vmem = pl.BlockSpec(memory_space=pltpu.VMEM)
    smem = pl.BlockSpec(memory_space=pltpu.SMEM)
    row = PAR * BLK
    dma = pltpu.SemaphoreType.DMA
    picture, grads = pl.pallas_call(
        functools.partial(kernel, tiles, cams, cap, channels),
        out_shape=(
            jax.ShapeDtypeStruct((channels, TPD * PIX), F32),
            jax.ShapeDtypeStruct((PAR, lanes), F32),
        ),
        in_specs=[vmem, vmem, smem, smem, vmem],
        out_specs=(vmem, vmem),
        scratch_shapes=[
            pltpu.VMEM((cams, PAR, lanes), F32),
            pltpu.VMEM((tiles, cap, blocks), BF16),
            pltpu.VMEM((tiles, cap, blocks), BF16),
            pltpu.VMEM((tiles, cap, row), BF16),
            pltpu.VMEM((tiles, cap, row), BF16),
            pltpu.VMEM((tiles, cap, row), BF16),
            pltpu.VMEM((tiles, cap, row), BF16),
            pltpu.VMEM((cams, PAR, lanes), F32),
            pltpu.VMEM((cams, PAR, lanes), F32),
            pltpu.VMEM((TPD * PAR, PIX), BF16),
            pltpu.VMEM((row, LANES), F32),
            pltpu.VMEM((ROWS, PIX), F32),
            pltpu.VMEM((ROWS, PIX), F32),
            pltpu.VMEM((ROWS, PIX), F32),
            dma((cams,)),
            dma((cams,)),
            dma((tiles,)),
            dma((tiles,)),
            dma((tiles,)),
            dma((tiles,)),
            dma((tiles,)),
            dma((tiles,)),
            dma((cams,)),
            dma((cams,)),
        ],
        compiler_params=pltpu.CompilerParams(
            collective_id=0, has_side_effects=True, vmem_limit_bytes=48 * 1024 * 1024
        ),
    )(params, ids, cam_linear, cam_shift, pix_grad.reshape(channels, TPD * PIX))
    return (
        picture.reshape(channels, 1, TPD * PIX),
        grads[GEO : GEO + 6],
        grads[:channels],
    )


def solution(mesh):
    return jax.shard_map(
        local,
        mesh=mesh,
        in_specs=(
            P(None, ("tiles", "cams")),
            P(None, ("tiles", "cams")),
            P(("tiles", "cams")),
            P(("tiles", "cams")),
            P(None, ("tiles", "cams")),
            P("cams", None),
            P("cams", None),
            P("cams", "tiles", None, None),
            P(None, "cams", "tiles"),
        ),
        out_specs=(
            P(None, "cams", "tiles"),
            P(None, ("tiles", "cams")),
            P(None, ("tiles", "cams")),
        ),
        check_vma=False,
    )
```

time: 148 us -> 33.5 us (0.23)
  waiting for transfers between devices: 38.9 us -> 0 us
  starting transfers between devices: 28.6 us -> 0 us
  Pallas kernels: 0 us -> 27.3 us
  local copies, waits for them, and re-layouts: 30.4 us -> 5.3 us
  other arithmetic: 18 us -> 0 us
  between operations: 15.9 us -> 0.72 us
  blocking collectives: 10.4 us -> 0 us
  matrix products: 4.99 us -> 0 us
    reduce_scatter x2 -> x0, waiting for transfers between devices: 30.7 us -> none  [the longest x1 21 us: local(): lax.psum_scatter(column_geometry, 'cams', scatter_dimension=1, tiled=True)]
    all_to_all x5 -> x0, starting transfers between devices: 28.5 us -> none  [the longest x1 7.25 us: local(): lax.all_to_all(request, 'tiles', split_axis=0, concat_axis=0, tiled=True)]
    pallas_call x0 -> x1, Pallas kernels: none -> 27.3 us  [local(): pl.pallas_call(functools.partial(kernel, tiles, cams, cap, channels), out...]
    all_gather x2 -> x0, blocking collectives: 10.4 us -> none  [the longest x1 5.21 us: local(): lax.all_gather(appearance, 'cams', axis=1, tiled=True)]
    all_to_all x5 -> x0, waiting for transfers between devices: 8.14 us -> none  [the longest x1 4.98 us: local(): lax.all_to_all(back_proj.reshape(6, -1), 'tiles', split_axis=1, concat_ax...]
    scatter x4 -> x0, local copies, waits for them, and re-layouts: 7.67 us -> none  [the longest x2 3.42 us: local(): back_proj = jnp.zeros((6, slot_count, BLK), jnp.bfloat16).at[:, entry_slo...]
    dot_general x4 -> x0, matrix products: 4.72 us -> none  [the longest x3 4.42 us: render_tile(): jnp.dot(colours, weight, precision=lax.Precision.HIGHEST, preferred_eleme...]
    another operation x4 -> x0, other arithmetic: 4.14 us -> none
  transfers between devices with their start and end apart: 7 -> 0, of which waited for: 4 -> 0; matrix products, arithmetic and copies ran while one was open for 28% -> 0% of each run, Pallas kernels for 0% -> 0%
where the time goes in v1:
time: 33.5 us; the launch traced here: 33.3 us
  Pallas kernels  27.3 us (81%)
  local copies, waits for them, and re-layouts  5.3 us (16%)
  between operations  0.72 us (2%)
    pallas_call x1, Pallas kernels, local(): pl.pallas_call(functools.partial(kernel, tiles, cams, cap, channels), out...  27.3 us
    unnamed x20, local copies, waits for them, and re-layouts  3.95 us

profile of v1, /device:TPU:0, one launch (start us, length us, event | category | flops | bytes accessed | tf_op | source)
XLA Modules:
  0.0 33.3 jit_solution(12032452280818540061)
XLA Ops:
  0.6 0.0 copy-start.4
  0.6 0.0 copy-start.3
  0.7 0.7 %copy-done.4 = s32[1,16,2,3]{1,2,3,0:T(2,128)S(1)} copy-done((s32[1,16,2,3]{1,2,3,0:T(2,128)S(1)}, s32[1,16,2,3]{1,2,3,0:T(2,128)}, u32[]{:S(2)}) %copy-start.4) | copy-done | bytes 408
  1.3 0.1 reshape.19
  1.4 0.0 copy-start.5
  1.4 0.0 copy-start.6
  1.4 0.0 copy-start.7
  1.5 0.0 copy-start.8
  1.5 0.0 copy-done.3
  1.5 0.6 %copy-done.5 = f32[2,256]{1,0:T(2,128)S(1)} copy-done((f32[2,256]{1,0:T(2,128)S(1)}, f32[2,256]{1,0:T(2,128)}, u32[]{:S(2)}) %copy-start.5) | copy-done | bytes 2072
  2.1 0.0 copy-done.6
  2.1 0.0 copy-done.7
  2.1 0.0 copy-done.8
  2.2 0.0 copy-start.1
  2.2 0.0 copy-start.2
  2.2 0.6 %copy-done.1 = f32[1,4]{1,0:T(1,128)S(1)} copy-done((f32[1,4]{1,0:T(1,128)S(1)}, f32[1,4]{1,0:T(1,128)}, u32[]{:S(2)}) %copy-start.1) | copy-done | bytes 40
  2.8 0.0 copy-done.2
  2.8 0.0 copy-start
  2.8 0.9 %copy-done = bf16[19,1,4096]{2,0,1:T(8,128)(2,1)S(1)} copy-done((bf16[19,1,4096]{2,0,1:T(8,128)(2,1)S(1)}, bf16[19,1,4096]{2,0,1:T(8,128)(2,1)}, u32[]{:S(2)}) %copy-start) | copy-done | bytes 155672
  3.8 27.3 %shard_map.112 = (f32[19,4096]{1,0:T(8,128)S(1)}, f32[32,256]{1,0:T(8,128)S(1)}) custom-call(f32[32,256]{1,0:T(8,128)S(1)} %concatenate.3.params_ref, s32[1,128]{1,0:T(1,128)S(1)} %pad.4.ids_ref, f32[1,4]{1,0:T(1,128)S(1)} %copy-done.1, f32[1,2]{1,0:T(1,128)S(1)} %copy-done.2, bf16[19,4096]{1,0:T(8,128)(2,1)S(1)} %bitcast.8), custom_call_target="tpu_custom_call" | custom-call | tf_op jit(solution)/shard_map/pallas_call | solution.py:404
  31.0 1.0 %copy.15 = f32[19,1,4096]{2,1,0:T(1,128)} copy(f32[19,1,4096]{2,0,1:T(8,128)S(1)} %bitcast.7) | data formatting | bytes 622592
  32.1 0.6 %slice.6 = f32[6,256]{1,0:T(8,128)} slice(f32[32,256]{1,0:T(8,128)S(1)} %get-tuple-element.6), slice={[24:30], [0:256]} | slice | bytes 12288 | tf_op jit(solution)/shard_map/slice | solution.py:444
  32.7 0.6 %slice.7 = f32[19,256]{1,0:T(8,128)} slice(f32[32,256]{1,0:T(8,128)S(1)} %get-tuple-element.6), slice={[0:19], [0:256]} | slice | bytes 38912 | tf_op jit(solution)/shard_map/slice | solution.py:445
  (6 shorter events, 0.1 us)
Async XLA Ops:
  0.6 0.7 %copy-start.4 = (s32[1,16,2,3]{1,2,3,0:T(2,128)S(1)}, s32[1,16,2,3]{1,2,3,0:T(2,128)}, u32[]{:S(2)}) copy-start(s32[1,16,2,3]{1,2,3,0:T(2,128)} %param.16) | copy-start | bytes 1156
  0.6 0.8 %copy-start.3 = (f32[19,256]{1,0:T(8,128)S(1)}, f32[19,256]{1,0:T(8,128)}, u32[]{:S(2)}) copy-start(f32[19,256]{1,0:T(8,128)} %param.13) | copy-start | bytes 58372
  1.4 0.7 %copy-start.5 = (f32[2,256]{1,0:T(2,128)S(1)}, f32[2,256]{1,0:T(2,128)}, u32[]{:S(2)}) copy-start(f32[2,256]{1,0:T(2,128)} %param.9) | copy-start | bytes 6148
  1.4 0.7 %copy-start.6 = (f32[2,256]{1,0:T(2,128)S(1)}, f32[2,256]{1,0:T(2,128)}, u32[]{:S(2)}) copy-start(f32[2,256]{1,0:T(2,128)} %param.10) | copy-start | bytes 6148
  1.4 0.7 %copy-start.7 = (f32[256]{0:T(256)S(1)}, f32[256]{0:T(256)}, u32[]{:S(2)}) copy-start(f32[256]{0:T(256)} %param.11) | copy-start | bytes 3076
  1.5 0.7 %copy-start.8 = (f32[256]{0:T(256)S(1)}, f32[256]{0:T(256)}, u32[]{:S(2)}) copy-start(f32[256]{0:T(256)} %param.12) | copy-start | bytes 3076
  2.2 0.7 %copy-start.1 = (f32[1,4]{1,0:T(1,128)S(1)}, f32[1,4]{1,0:T(1,128)}, u32[]{:S(2)}) copy-start(f32[1,4]{1,0:T(1,128)} %linear_ref.1) | copy-start | bytes 52
  2.2 0.7 %copy-start.2 = (f32[1,2]{1,0:T(1,128)S(1)}, f32[1,2]{1,0:T(1,128)}, u32[]{:S(2)}) copy-start(f32[1,2]{1,0:T(1,128)} %shift_ref.1) | copy-start | bytes 28
  2.8 0.9 %copy-start = (bf16[19,1,4096]{2,0,1:T(8,128)(2,1)S(1)}, bf16[19,1,4096]{2,0,1:T(8,128)(2,1)}, u32[]{:S(2)}) copy-start(bf16[19,1,4096]{2,0,1:T(8,128)(2,1)} %param.17) | copy-start | bytes 466948

commit v2 on v1

--- a/solution.py
+++ b/solution.py
@@ -72,13 +72,41 @@
     cams,
     cap,
     feat,
-    params_ref,
-    ids_ref,
+    *refs,
+):
+    hbm_in = refs[:9]
+    picture_ref, geometry_ref, appearance_ref = refs[9:12]
+    held_in = refs[12:21]
+    offsets_ref, diag_ref, lower_ref, logit_ref, looks_ref = held_in[:5]
+    linear_ref, shift_ref, lists_ref, cot_ref = held_in[5:]
+    body(
+        tiles, cams, cap, feat, hbm_in, held_in, offsets_ref, diag_ref, lower_ref, logit_ref,
+        looks_ref, linear_ref, shift_ref, lists_ref, cot_ref, picture_ref, geometry_ref,
+        appearance_ref, *refs[21:]
+    )
+
+
+def body(
+    tiles,
+    cams,
+    cap,
+    feat,
+    hbm_in,
+    held_in,
+    offsets_ref,
+    diag_ref,
+    lower_ref,
+    logit_ref,
+    looks_ref,
     linear_ref,
     shift_ref,
+    lists_ref,
     cot_ref,
     picture_ref,
-    grads_ref,
+    geometry_ref,
+    appearance_ref,
+    load_sem,
+    params_ref,
     column,
     request_out,
     request_in,
@@ -131,7 +159,19 @@
     lax.fori_loop(1, tiles, greet_tiles, 0)
     lax.fori_loop(1, cams, greet_cams, 0)
 
-    ids = ids_ref[...]
+    loads = [
+        pltpu.make_async_copy(source, target, load_sem.at[i])
+        for i, (source, target) in enumerate(zip(hbm_in, held_in))
+    ]
+    for i in (7, 0, 1, 2, 3, 4, 5, 6, 8):
+        loads[i].start()
+
+    loads[7].wait()
+    ids = jnp.concatenate(
+        [lists_ref[l, d : d + 1, :] for d in range(2) for l in range(LIST)]
+        + [jnp.full((1, LANES - 2 * LIST * TPD), -1, jnp.int32)],
+        axis=1,
+    )
     entry_column = lax.div(ids, jnp.int32(blocks))
     in_column = ids - entry_column * blocks
     entry_column = jnp.where(ids < 0, -1, entry_column)
@@ -180,12 +220,23 @@
         sums_out.at[turn(cam, k, cams)], sums_in.at[cam], k, send_sum, recv_sum
     )
 
+    for i in range(5):
+        loads[i].wait()
+    looks = looks_ref[...]
+    geometry = jnp.concatenate(
+        [offsets_ref[...], diag_ref[...], lower_ref[...], logit_ref[...], jnp.zeros((2, lanes), F32)],
+        axis=0,
+    )
+    params_ref[...] = jnp.concatenate(
+        [looks, jnp.zeros((GEO - feat, lanes), F32), *split(geometry)], axis=0
+    ).astype(BF16)
     pl.semaphore_wait(barrier, tiles - 1 + cams - 1)
     over(cams, copy_params, "start")
     over(tiles, copy_request, "start")
     column[cam] = params_ref[...]
     request_in[tile] = request_out[tile]
 
+    loads[8].wait()
     fill = jnp.zeros((PAR - feat, PIX), F32)
     for t in range(TPD):
         part = cot_ref[:, t * PIX : (t + 1) * PIX].astype(F32)
@@ -205,14 +256,15 @@
         (iota((PAR, TPD * PAR), 1) & (PAR - 1)) == iota((PAR, TPD * PAR), 0), 1.0, 0.0
     ).astype(BF16)
 
+    loads[5].wait()
+    loads[6].wait()
     over(cams, copy_params, "wait_recv")
     split_rows = GEO + 3 * (PAR - GEO)
     in_block = iota((split_rows, BLK, lanes), 2) & (BLK - 1)
     in_place = in_block == iota((split_rows, BLK, lanes), 1)
     table = jnp.zeros((split_rows * BLK, blocks), F32)
     for c in range(cams):
-        piece = column[c]
-        stacked = jnp.concatenate([piece[:GEO], *split(piece[GEO:])], axis=0)
+        stacked = column[c].astype(F32)
         apart = jnp.where(in_place, jnp.broadcast_to(stacked[:, None, :], in_place.shape), 0.0)
         apart = apart.reshape(split_rows * BLK, lanes).astype(BF16)
         to_block = jnp.where(
@@ -229,8 +281,8 @@
         + table[base + 2 * geo_rows :]
     )
     geometry = [geometry[r * BLK : (r + 1) * BLK] for r in range(6)]
-    linear = [linear_ref[0, i] for i in range(4)]
-    camera_shift = [shift_ref[0, i] for i in range(2)]
+    linear = [linear_ref[:, i : i + 1] for i in range(4)]
+    camera_shift = [shift_ref[:, i : i + 1] for i in range(2)]
     projected, pull_params = jax.vjp(lambda *rows: project(*rows, linear, camera_shift), *geometry)
     table = jnp.concatenate(
         [table[:base], *projected, jnp.zeros((2 * BLK, blocks), F32)], axis=0
@@ -328,7 +380,7 @@
     masked = jnp.where(same_tile, jnp.broadcast_to(copies[None], (TPD, PAR, ROWS)), 0.0)
     picture = dot(masked.reshape(TPD * PAR, ROWS).astype(BF16), shares, NN)
     for t in range(TPD):
-        picture_ref[:, t * PIX : (t + 1) * PIX] = picture[t * PAR : t * PAR + feat]
+        picture_ref[:, 0, t * PIX : (t + 1) * PIX] = picture[t * PAR : t * PAR + feat]
 
     over(tiles, copy_back, "wait_recv")
     summed = dot(back_in[...].reshape(slots, PAR * BLK), wanted, TN)
@@ -357,13 +409,24 @@
     over(cams, copy_sums, "start")
     sums_in[cam] = sums_out[cam]
     over(cams, copy_sums, "wait_recv")
-    grads_ref[...] = jnp.sum(sums_in[...], axis=0)
+    total = jnp.sum(sums_in[...], axis=0)
+    geometry_ref[...] = total[GEO : GEO + 6]
+    appearance_ref[...] = total[:feat]
 
     over(cams, copy_params, "wait_send")
     over(tiles, copy_request, "wait_send")
     over(tiles, copy_table, "wait_send")
     over(tiles, copy_back, "wait_send")
     over(cams, copy_sums, "wait_send")
+
+
+def store(*refs):
+    sems = refs[6]
+    copies = [pltpu.make_async_copy(refs[i], refs[3 + i], sems.at[i]) for i in range(3)]
+    for copy in copies:
+        copy.start()
+    for copy in copies:
+        copy.wait()
 
 
 def local(
@@ -383,34 +446,36 @@
     lanes = offsets.shape[1]
     blocks = cams * lanes // BLK
     cap = -(-(4 * TPD * LIST // tiles) // 16) * 16
-    params = jnp.concatenate(
-        [
-            appearance,
-            jnp.zeros((GEO - channels, lanes), F32),
-            offsets,
-            factor_diag,
-            factor_off[None, :],
-            logit[None, :],
-            jnp.zeros((PAR - GEO - 6, lanes), F32),
-        ],
-        axis=0,
-    )
-    ids = block_lists.reshape(TPD, 2 * LIST).T.reshape(1, TPD * 2 * LIST)
-    ids = jnp.pad(ids, ((0, 0), (0, LANES - ids.shape[1])), constant_values=-1)
     vmem = pl.BlockSpec(memory_space=pltpu.VMEM)
-    smem = pl.BlockSpec(memory_space=pltpu.SMEM)
+    hbm = pl.BlockSpec(memory_space=pltpu.HBM)
+    arrays = (
+        offsets,
+        factor_diag,
+        factor_off[None, :],
+        logit[None, :],
+        appearance,
+        cam_linear,
+        cam_shift,
+        block_lists.transpose(0, 3, 2, 1).reshape(LIST, 2, TPD),
+        pix_grad.reshape(channels, TPD * PIX),
+    )
+    split_rows = GEO + 3 * (PAR - GEO)
     row = PAR * BLK
     dma = pltpu.SemaphoreType.DMA
-    picture, grads = pl.pallas_call(
+    results = pl.pallas_call(
         functools.partial(kernel, tiles, cams, cap, channels),
         out_shape=(
-            jax.ShapeDtypeStruct((channels, TPD * PIX), F32),
-            jax.ShapeDtypeStruct((PAR, lanes), F32),
+            jax.ShapeDtypeStruct((channels, 1, TPD * PIX), F32),
+            jax.ShapeDtypeStruct((6, lanes), F32),
+            jax.ShapeDtypeStruct((channels, lanes), F32),
         ),
-        in_specs=[vmem, vmem, smem, smem, vmem],
-        out_specs=(vmem, vmem),
+        in_specs=[hbm] * len(arrays),
+        out_specs=(vmem,) * 3,
         scratch_shapes=[
-            pltpu.VMEM((cams, PAR, lanes), F32),
+            *[pltpu.VMEM(array.shape, array.dtype) for array in arrays],
+            dma((len(arrays),)),
+            pltpu.VMEM((split_rows, lanes), BF16),
+            pltpu.VMEM((cams, split_rows, lanes), BF16),
             pltpu.VMEM((tiles, cap, blocks), BF16),
             pltpu.VMEM((tiles, cap, blocks), BF16),
             pltpu.VMEM((tiles, cap, row), BF16),
@@ -436,14 +501,16 @@
             dma((cams,)),
         ],
         compiler_params=pltpu.CompilerParams(
-            collective_id=0, has_side_effects=True, vmem_limit_bytes=48 * 1024 * 1024
+            collective_id=0, has_side_effects=True, vmem_limit_bytes=64 * 1024 * 1024
         ),
-    )(params, ids, cam_linear, cam_shift, pix_grad.reshape(channels, TPD * PIX))
-    return (
-        picture.reshape(channels, 1, TPD * PIX),
-        grads[GEO : GEO + 6],
-        grads[:channels],
-    )
+    )(*arrays)
+    return pl.pallas_call(
+        store,
+        out_shape=tuple(jax.ShapeDtypeStruct(r.shape, r.dtype) for r in results),
+        in_specs=[vmem] * 3,
+        out_specs=(hbm,) * 3,
+        scratch_shapes=[dma((3,))],
+    )(*results)
 
 
 def solution(mesh):

time: 33.5 us -> 30.1 us (0.90)
  local copies, waits for them, and re-layouts: 5.3 us -> 0 us
  Pallas kernels: 27.3 us -> 29.3 us
    unnamed x20 -> x0, local copies, waits for them, and re-layouts: 3.95 us -> none
    pallas_call x0 -> x1, Pallas kernels: none -> 1.73 us  [local(): pl.pallas_call(store, out_shape=tuple((jax.ShapeDtypeStruct(r.shape, r.dt...]
    slice x2 -> x0, local copies, waits for them, and re-layouts: 1.21 us -> none  [the longest x1 0.61 us: local(): grads[:channels]]
where the time goes in v2:
time: 30.1 us; the launch traced here: 29.9 us
  Pallas kernels  29.3 us (97%)
  between operations  0.64 us (2%)
    pallas_call x1, Pallas kernels, local(): pl.pallas_call(functools.partial(kernel, tiles, cams, cap, channels), out...  27.5 us
    pallas_call x1, Pallas kernels, local(): pl.pallas_call(store, out_shape=tuple((jax.ShapeDtypeStruct(r.shape, r.dt...  1.73 us

profile of v2, /device:TPU:0, one launch (start us, length us, event | category | flops | bytes accessed | tf_op | source)
XLA Modules:
  0.0 29.9 jit_solution(12410780322857548314)
XLA Ops:
  0.6 27.5 %shard_map.112 = (f32[19,1,4096]{2,1,0:T(1,128)}, f32[6,256]{1,0:T(8,128)}, f32[19,256]{1,0:T(8,128)}) custom-call(f32[2,256]{1,0:T(2,128)} %refs_0_.1, f32[2,256]{1,0:T(2,128)} %refs_1_.1, f32[1,256]{1,0:T(1,128)} %bitcast.8, f32[1,256]{1,0:T(1,128)} %bitcast.9, f32[19,256]{1,0:T(8,128)} %refs_4_.1, f32[1,4]{1,0:T(1,128)} %refs_5_.1, f32[1,2]{1,0:T(1,128)} %refs_6_.1, ...), custom_call_target="tpu_custom_call" | custom-call | tf_op jit(solution)/shard_map/pallas_call | solution.py:465
  28.2 1.7 %shard_map.113 = (f32[19,1,4096]{2,1,0:T(1,128)}, f32[6,256]{1,0:T(8,128)}, f32[19,256]{1,0:T(8,128)}) custom-call(f32[19,1,4096]{2,1,0:T(1,128)} %get-tuple-element.6.refs_0_, f32[6,256]{1,0:T(8,128)} %get-tuple-element.7.refs_1_, f32[19,256]{1,0:T(8,128)} %get-tuple-element.8.refs_2_), custom_call_target="tpu_custom_call" | custom-call | tf_op jit(solution)/shard_map/pallas_call | solution.py:507
